TPU v7x, 256 devices: a whole 4x4x8 slice. The times are simulated.
256 devices in a mesh: gz: 32 (over x, y, core), gy: 8 (over z).
Axes of the slice: x: 4, y: 4, z: 8, core: 2. Of those that a mesh axis runs over, the one named last changes fastest.
Arguments:
- velocity: float32 [3, 512, 256, 512], P(None, 'gz', 'gy'), may hold values from -5 to 8
- diffusion: float32 [256, 512], P('gy'), may hold values from 0.5 to 1000
- wall_types: int32 [256, 512], P('gy'), may hold values from 0 to 3
- stretch_index: int32 [512], replicated, may hold values from 0 to 6
- bulk_target: float32 [1], replicated, may hold values from 0.5 to 1.5
Outputs:
- velocity_out: float32 [3, 512, 256, 512], P(None, 'gz', 'gy')
All inputs are finite; a program needn't handle non-finite values.
Results may differ from a plain program's by a relative error of at most 0.0028.
Values sent between devices are 32-bit elements; how exact they have to be, the bound alone decides.
A program may use at most 192 MiB of HBM per device.

v0:
```python
import jax
import jax.numpy as jnp
from jax import lax
from jax.sharding import PartitionSpec as P


def from_behind(block, axis, distance):
    devices = range(lax.axis_size(axis))
    route = [(i - distance, i) for i in devices if i - distance in devices]
    return lax.ppermute(block, axis, route)


def spacing(stretch_index):
    return 0.5 + 0.25 * stretch_index.astype(jnp.float32)


def face_tables(heights):
    faces = 2.0 / (heights[:-1] + heights[1:])
    padding = jnp.zeros((1,), jnp.float32)
    return (jnp.concatenate([padding, faces]), jnp.concatenate([faces, padding]))


def cell_rows(heights, face_left, face_right, is_first, is_last, diffusion, lower_wall, upper_wall):
    left_sum = face_left + is_first * lower_wall
    right_sum = face_right + is_last * upper_wall
    diagonal = heights + diffusion * (left_sum + right_sum)
    return (-diffusion * face_left, diagonal, -diffusion * face_right)


def scan_thomas(lower_band, diagonal, upper_band, rhs_rows):

    def forward(carry, row_data):
        ratio_prev, value_prev = carry
        low_row, diag_row, upper_row, right_row = row_data
        divisor = diag_row - low_row * ratio_prev
        factor = upper_row / divisor
        solved_row = (right_row - low_row[None] * value_prev) / divisor[None]
        return ((factor, solved_row), (factor, solved_row))

    zero_state = (
        jnp.zeros(diagonal.shape[1:], jnp.float32),
        jnp.zeros(rhs_rows.shape[1:], jnp.float32),
    )
    _, (factors, values) = lax.scan(
        forward, zero_state, (lower_band, diagonal, upper_band, rhs_rows)
    )

    def backward(following, row_data):
        factor, solved_row = row_data
        current = solved_row - factor[None] * following
        return (current, current)

    _, solved = lax.scan(
        backward, jnp.zeros(rhs_rows.shape[1:], jnp.float32), (factors, values), reverse=True
    )
    return solved


def corrected(streamwise, potential, heights, bulk_target, volume):
    partial_flow = jnp.sum(heights[:, None, None] * streamwise)
    partial_weight = jnp.sum(heights[:, None, None] * potential)
    flow_total, weight_total = lax.psum((partial_flow, partial_weight), ("gz", "gy"))
    return streamwise + (bulk_target[0] * volume - flow_total) / weight_total * potential


def shards(velocity, diffusion, wall_types, stretch_index, bulk_target):
    position = lax.axis_index("gz")
    devices_z = lax.axis_size("gz")
    local_cells = velocity.shape[1]
    lines_y = velocity.shape[2]
    lines_x = velocity.shape[3]
    cells_total = local_cells * devices_z
    heights_all = spacing(stretch_index)
    left_all, right_all = face_tables(heights_all)
    volume = jnp.sum(heights_all) * (lines_y * lax.axis_size("gy")) * lines_x
    bottom_flag = (wall_types % 2).astype(jnp.float32)
    top_flag = (wall_types // 2).astype(jnp.float32)
    lower_wall = bottom_flag * (2.0 / heights_all[0])
    upper_wall = top_flag * (2.0 / heights_all[cells_total - 1])
    offset = position * local_cells
    heights = lax.dynamic_slice_in_dim(heights_all, offset, local_cells)
    face_left = lax.dynamic_slice_in_dim(left_all, offset, local_cells)
    face_right = lax.dynamic_slice_in_dim(right_all, offset, local_cells)
    cell_ids = offset + jnp.arange(local_cells, dtype=jnp.int32)
    is_first = (cell_ids == 0).astype(jnp.float32)
    is_last = (cell_ids == cells_total - 1).astype(jnp.float32)
    lower_band, diagonal, upper_band = cell_rows(
        heights[:, None, None],
        face_left[:, None, None],
        face_right[:, None, None],
        is_first[:, None, None],
        is_last[:, None, None],
        diffusion[None],
        lower_wall[None],
        upper_wall[None],
    )
    unit_part = jnp.broadcast_to(heights[:, None, None, None], (local_cells, 1, lines_y, lines_x))
    rhs_rows = jnp.concatenate(
        [heights[:, None, None, None] * jnp.moveaxis(velocity, 0, 1), unit_part], axis=1
    )
    inner_count = local_cells - 1
    couple_left = jnp.concatenate(
        [
            (-lower_band[0])[None, None],
            jnp.zeros((inner_count - 1, 1, lines_y, lines_x), jnp.float32),
        ],
        axis=0,
    )
    couple_right = jnp.concatenate(
        [
            jnp.zeros((inner_count - 1, 1, lines_y, lines_x), jnp.float32),
            (-upper_band[inner_count - 1])[None, None],
        ],
        axis=0,
    )
    inner_rhs = jnp.concatenate([rhs_rows[:inner_count], couple_left, couple_right], axis=1)
    keep_upper = (jnp.arange(inner_count, dtype=jnp.int32) < inner_count - 1).astype(jnp.float32)
    inner_upper = upper_band[:inner_count] * keep_upper[:, None, None]
    interior = scan_thomas(lower_band[:inner_count], diagonal[:inner_count], inner_upper, inner_rhs)
    neighbour = from_behind(interior[0], "gz", -1)
    last_row = interior[inner_count - 1]
    edge_lower = lower_band[local_cells - 1]
    edge_diagonal = diagonal[local_cells - 1]
    edge_upper = upper_band[local_cells - 1]
    reduced_lower = edge_lower * last_row[4]
    reduced_diagonal = edge_lower * last_row[5] + edge_diagonal + edge_upper * neighbour[4]
    reduced_upper = edge_upper * neighbour[5]
    reduced_rhs = (
        rhs_rows[local_cells - 1]
        - edge_lower[None] * last_row[:4]
        - edge_upper[None] * neighbour[:4]
    )
    reduced = jnp.concatenate(
        [reduced_lower[None], reduced_diagonal[None], reduced_upper[None], reduced_rhs], axis=0
    )
    gathered = lax.all_gather(reduced[None], "gz", axis=0, tiled=True)
    solved_all = scan_thomas(gathered[:, 0], gathered[:, 1], gathered[:, 2], gathered[:, 3:])
    own_value = lax.dynamic_index_in_dim(solved_all, position, 0, keepdims=False)
    prev_value = lax.dynamic_index_in_dim(
        solved_all, jnp.maximum(position - 1, 0), 0, keepdims=False
    ) * (position > 0).astype(jnp.float32)
    inner_values = (
        interior[:, :4] + interior[:, 4:5] * prev_value[None] + interior[:, 5:6] * own_value[None]
    )
    complete = jnp.concatenate([inner_values, own_value[None]], axis=0)
    streamwise = corrected(complete[:, 0], complete[:, 3], heights, bulk_target, volume)
    return jnp.stack([streamwise, complete[:, 1], complete[:, 2]], axis=0)


def solution(mesh):
    return jax.shard_map(
        shards,
        mesh=mesh,
        in_specs=(P(None, "gz", "gy", None), P("gy", None), P("gy", None), P(), P()),
        out_specs=P(None, "gz", "gy", None),
        check_vma=False,
    )
```

profile of v0, /device:TPU:1, one launch (start us, length us, event | category | flops | bytes accessed | tf_op | source)
XLA Modules:
  0.0 542.6 jit_solution(6015699799836812309)
XLA Ops:
  11.9 2.4 broadcast_multiply_fusion
  16.5 2.5 fusion.5
  21.9 2.8 select_maximum_fusion
  24.7 3.3 broadcast.84.clone
  28.0 56.0 %while.68 = (s32[]{:T(128)}, f32[32,512]{1,0:T(8,128)}, f32[6,32,512]{2,1,0:T(8,128)}, f32[15,32,512]{2,1,0:T(8,128)}, f32[15,6,32,512]{3,2,1,0:T(8,128)}, /*ind...) while((s32[]{:T(128)}, f32[32,512]{1,0:T(8,128)}, ...), condition=%wide.region_1.2_spmd.clone, body=%wide.region_0.0_spmd.clone.sunk | while | flops 458755 | bytes 2229368 | solution.py:44
  36.9 2.1 bitcast_dynamic-update-slice_fusion.13
  48.1 2.2 bitcast_dynamic-update-slice_fusion.13
  51.9 2.2 bitcast_dynamic-update-slice_fusion.13
  55.7 2.2 bitcast_dynamic-update-slice_fusion.13
  78.1 2.2 bitcast_dynamic-update-slice_fusion.13
  84.0 3.3 broadcast.84
  87.4 52.1 %while.69 = (s32[]{:T(128)}, f32[6,32,512]{2,1,0:T(8,128)S(1)}, f32[15,6,32,512]{3,2,1,0:T(8,128)}, f32[15,6,32,512]{3,2,1,0:T(8,128)}, f32[15,32,512]{2,1,0:T(8,128)}, /*index=5*/s32[]{:T(128)}, s32[]{:T(128)}, s32[]{:T(128)}) while((s32[]{:T(128)}, f32[6,32,512]{2,1,0:T(8,128)S(1)}, f32[15,6,32,512]{3,2,1,0:T(8,128)}, ...), condition=%wide.region_3.4_spmd.clone, body=%wide.region_2.3_spmd.clone.sunk | while | flops 294916 | bytes 1769587 | solution.py:53
  140.4 5.1 collective-permute-start
  145.6 4.9 collective-permute-done
  156.5 74.6 %all-gather.3.cloned.1.call-done = f32[224,32,512]{2,1,0:T(8,128)} async-done(((f32[7,32,512]{2,1,0:T(8,128)}), f32[224,32,512]{2,1,0:T(8,128)}) %all-gather.3.cloned.1.call-update) | async-done | bytes 14680080 | tf_op jit(solution)/shard_map/all_gather | solution.py:136
  231.1 8.5 %slice.155 = f32[32,4,32,512]{3,2,1,0:T(8,128)} slice(f32[32,7,32,512]{3,2,1,0:T(8,128)} %bitcast.131), slice={[0:32], [3:7], [0:32], [0:512]} | slice | bytes 16777216 | tf_op jit(solution)/shard_map/slice | solution.py:137
  239.6 6.0 %slice_bitcast_fusion = (f32[32,32,512]{2,1,0:T(8,128)}, f32[32,32,512]{2,1,0:T(8,128)}, f32[32,32,512]{2,1,0:T(8,128)}) fusion(f32[32,7,32,512]{3,2,1,0:T(8,128)} %bitcast.132), kind=kLoop, calls=%fused_computation.46 | loop fusion | bytes 12582912 | tf_op jit(solution)/shard_map/squeeze | solution.py:137
  245.6 4.4 broadcast.92.clone
  250.0 106.1 %while.70 = (s32[]{:T(128)}, f32[32,512]{1,0:T(8,128)S(1)}, f32[4,32,512]{2,1,0:T(8,128)S(1)}, f32[32,32,512]{2,1,0:T(8,128)}, f32[32,4,32,512]{3,2,1,0:T(8,128)...) while((s32[]{:T(128)}, f32[32,512]{1,0:T(8,128)S(1)}, ...), condition=%wide.region_5.6_spmd.clone, body=%wide.region_4.5_spmd.clone.sunk | while | flops 327683 | bytes 1705080 | solution.py:44
  356.1 4.3 broadcast.92
  360.4 84.8 %while.71 = (s32[]{:T(128)}, f32[4,32,512]{2,1,0:T(8,128)S(1)}, f32[32,4,32,512]{3,2,1,0:T(8,128)}, f32[32,4,32,512]{3,2,1,0:T(8,128)}, f32[32,32,512]{2,1,0:T(8,128)}, /*index=5*/s32[]{:T(128)}, s32[]{:T(128)}, s32[]{:T(128)}) while((s32[]{:T(128)}, f32[4,32,512]{2,1,0:T(8,128)S(1)}, f32[32,4,32,512]{3,2,1,0:T(8,128)}, ...), condition=%wide.region_7.8_spmd.clone, body=%wide.region_6.7_spmd.clone.sunk | while | flops 196612 | bytes 1245299 | solution.py:53
  448.2 2.9 fusion.4
  454.1 75.8 %all-reduce.2 = (f32[]{:T(128)}, f32[]{:T(128)}) all-reduce(f32[]{:T(128)} %get-tuple-element.410, f32[]{:T(128)} %get-tuple-element.409), channel_id=1, replica_groups=mesh['gz'=32,'gy'=8] {'gz','gy'}, use_global_device_ids=true, to_apply=%region_10.11 | all-reduce | flops 2 | bytes 16 | tf_op jit(solution)/shard_map/psum | solution.py:62
  531.2 2.6 add_bitcast_fusion
  (235 shorter events, 310.6 us)
Async XLA Ops:
  6.5 224.5 %all-gather.3.cloned.1.call-start = ((), (), s32[]{:S(2)}) async-start(), calls=%async_computation | async-start | bytes 15138816 | tf_op jit(solution)/shard_map/all_gather | solution.py:136
  14.4 1.0 copy-start.2
  14.4 2.1 copy-start.3
  16.4 3.7 copy-start.5
  16.5 2.6 copy-start.4
  20.1 1.7 copy-start.6
  21.3 3.4 copy-start.1
  140.4 10.0 %collective-permute-start = (f32[6,32,512]{2,1,0:T(8,128)S(1)}, f32[6,32,512]{2,1,0:T(8,128)S(1)}, u32[]{:S(2)}, u32[]{:S(2)}) collective-permute-start(f32[6,32,512]{2,1,0:T(8,128)S(1)} %slice_bitcast_fusion.5), channel_id=1, source_target_pairs={{8,0},{16,8},{24,16},{32,24},{40,32},{48,40},{56,48},{64,56},{72,6... | collective-permute-start | bytes 1179656 | tf_op jit(solution)/shard_map/ppermute | solution.py:10
  451.1 1.9 copy-start
Sparse Core Ops, SparseCore 0:
  153.6 77.4 all-gather.2
where the time goes:
time: 550 us; the launch traced here: 543 us
  other arithmetic  276 us (50%)
  local copies, waits for them, and re-layouts  88.7 us (16%)
  waiting for transfers between devices  79.5 us (14%)
  blocking collectives  75.8 us (14%)
  between operations  17.5 us (3%)
    dynamic_update_slice x141, other arithmetic, scan_thomas(): lax.scan(forward, zero_state, (lower_band, diagonal, upper_band, rhs_rows))  250 us
    psum x1, blocking collectives, corrected(): lax.psum((partial_flow, partial_weight), ('gz', 'gy'))  75.8 us
    all_gather x1, waiting for transfers between devices, shards(): gathered = lax.all_gather(reduced[None], 'gz', axis=0, tiled=True)  74.6 us
    mul x47, local copies, waits for them, and re-layouts, backward(): current = solved_row - factor[None] * following  48.9 us
    another operation x4, local copies, waits for them, and re-layouts  15.4 us
  transfers between devices with their start and end apart: 2, of which 2 were waited for; matrix products, arithmetic and copies ran while one was open for 0% of the time, Pallas kernels for 0%

commit v1 on v0

v1 whole, which is shorter than its diff:
```python
import jax
import jax.numpy as jnp
from jax import lax
from jax.experimental import pallas as pl
from jax.experimental.pallas import tpu as pltpu
from jax.sharding import PartitionSpec as P

MESH = pl.DeviceIdType.MESH
F32 = jnp.float32
BLOCKS = 32
PLANES = 8
CELLS = 16
INNER = CELLS - 1
ROWS = 32
LANES = 512
TILES = LANES // 128
MSG = 24


def inverse(x):
    guess = pl.reciprocal(x, approx=True)
    return guess * (2.0 - x * guess)


def wide(tile):
    row = jnp.concatenate([tile] * TILES, axis=1)
    return jnp.concatenate([row] * (ROWS // 8), axis=0)


def across(column):
    return jnp.concatenate([column] * TILES, axis=1)


def tiles_of():
    return [(a, b) for a in range(ROWS // 8) for b in range(TILES)]


def part(x, a, b):
    return x[a * 8:(a + 1) * 8, b * 128:(b + 1) * 128]


def reduce_kernel(velocity, diffusion, walls, stretch, bulk,
                  p_ref, l_ref, r_ref, ret_ref, tbuf_ref, fix_ref,
                  v_ref, d_ref, wall_ref, stretch_ref, bulk_ref, w_ref, inv_ref, hb_ref,
                  fsend, frecv, al_ref, be_ref, dh_ref, im_ref, a_ref, g_ref, t_ref, z_ref, y_ref,
                  tsend, rsend, flow_out, flow_in, plane_out, plane_in,
                  load_sem, v_sem, send_sem, recv_sem):
    me = lax.axis_index("gz")
    plane = lax.axis_index("gy")

    def load(src, dst, sem):
        copy = pltpu.make_async_copy(src, dst, sem)
        copy.start()
        return copy

    stretch_load = load(stretch, stretch_ref, load_sem.at[0])
    bulk_load = load(bulk, bulk_ref, load_sem.at[1])
    d_load = load(diffusion, d_ref, load_sem.at[2])
    wall_load = load(walls, wall_ref, load_sem.at[3])
    v_loads = [load(velocity.at[c], v_ref.at[c], v_sem.at[c]) for c in range(3)]

    barrier = pltpu.get_barrier_semaphore()

    def greet(step, carry):
        pl.semaphore_signal(barrier, 1, device_id={"gz": lax.rem(me + step, BLOCKS)}, device_id_type=MESH)
        return carry

    def greet_plane(step, carry):
        pl.semaphore_signal(barrier, 1, device_id={"gy": lax.rem(plane + step, PLANES)}, device_id_type=MESH)
        return carry

    lax.fori_loop(1, BLOCKS, greet, 0)
    lax.fori_loop(1, PLANES, greet_plane, 0)

    stretch_load.wait()
    bulk_load.wait()

    def height(cell):
        return 0.5 + 0.25 * stretch_ref[cell].astype(F32)

    def table_row(block, carry):
        for k in range(CELLS):
            hb_ref[k, pl.ds(block, 1), :] = jnp.full((1, 128), height(block * CELLS + k), F32)
        return carry

    lax.fori_loop(0, BLOCKS, table_row, 0)

    first = me * CELLS
    h = [height(first + k) for k in range(CELLS)]
    below = height(jnp.maximum(first - 1, 0))
    above = height(jnp.minimum(first + CELLS, BLOCKS * CELLS - 1))

    def face(one, other):
        return 2.0 * inverse(jnp.full((8, 128), one + other, F32))

    ends = [below] + h
    f = [wide(face(ends[k], ends[k + 1])) for k in range(CELLS)]
    floor_scale = 2.0 * inverse(jnp.full((8, 128), height(0), F32))
    roof_scale = 2.0 * inverse(jnp.full((8, 128), height(BLOCKS * CELLS - 1), F32))
    d_load.wait()
    wall_load.wait()
    d = d_ref[...]
    lower_wall = (wall_ref[...] & 1).astype(F32) * wide(floor_scale)
    f[0] = jnp.where(me == 0, lower_wall, f[0])

    w = None
    q = d * f[0]
    for k in range(INNER):
        low, high = d * f[k], d * f[k + 1]
        pivot = h[k] + (low + high)
        if k:
            pivot = pivot - low * w
        inv = inverse(pivot)
        w = high * inv
        inv_ref[k] = inv
        w_ref[k] = w
        l_ref[k] = q * inv
        q = q * w
    left, right = l_ref[INNER - 1], w
    r_ref[INNER - 1] = right
    for k in range(INNER - 2, -1, -1):
        w = w_ref[k]
        left = l_ref[k] + w * left
        right = w * right
        l_ref[k] = left
        r_ref[k] = right

    edge_low, edge_high = d * f[0], d * f[INNER]
    total = jnp.zeros((ROWS, LANES), F32)
    for c in range(3):
        v_loads[c].wait()
        y = None
        for k in range(INNER):
            rhs = h[k] * v_ref[c, k]
            if c == 0:
                total = total + rhs
            y = rhs if k == 0 else rhs + w_ref[k - 1] * y
            p_ref[c, k] = y
        x = inv_ref[INNER - 1] * y
        p_ref[c, INNER - 1] = x
        own = h[INNER] * v_ref[c, INNER]
        if c == 0:
            total = total + own
        own = own + edge_high * x
        for k in range(INNER - 2, -1, -1):
            x = inv_ref[k] * p_ref[c, k] + w_ref[k] * x
            p_ref[c, k] = x
        other = edge_low * x
        for a, b in tiles_of():
            at = a * 8 * MSG + b
            own_row, other_row = (c * 4, 8 + c * 4) if c < 2 else (16, 20)
            fsend[pl.ds(at + own_row, 8, stride=MSG), :] = part(own, a, b)
            fsend[pl.ds(at + other_row, 8, stride=MSG), :] = part(other, a, b)
    local = jnp.zeros((8, 128), F32)
    for a, b in tiles_of():
        local = local + part(total, a, b)

    def send_all(src, dst, rows, which):
        def one(step, carry):
            peer = lax.rem(me + step, BLOCKS)
            pltpu.make_async_remote_copy(
                src_ref=src.at[pl.ds(pl.multiple_of(peer * rows, rows), rows)],
                dst_ref=dst.at[pl.ds(pl.multiple_of(me * rows, rows), rows)],
                send_sem=send_sem.at[which], recv_sem=recv_sem.at[which],
                device_id={"gz": peer}, device_id_type=MESH).start()
            return carry
        lax.fori_loop(1, BLOCKS, one, 0)
        mine = pl.ds(pl.multiple_of(me * rows, rows), rows)
        dst[mine] = src[mine]

    def wait_all(ref, rows, sem):
        span = ref.at[pl.ds(0, (BLOCKS - 1) * rows)]
        pltpu.make_async_copy(span, span, sem).wait()

    pl.semaphore_wait(barrier, BLOCKS - 1 + PLANES - 1)
    send_all(fsend, frecv, MSG, 0)

    block_id = lax.broadcasted_iota(jnp.int32, (BLOCKS, LANES), 0)
    heights = [hb_ref[k] for k in range(CELLS)]
    before = pltpu.roll(heights[INNER], 1, 0)
    after = pltpu.roll(heights[0], BLOCKS - 1, 0)
    ends = [before] + heights + [after]
    faces = [across(2.0 * inverse(ends[k] + ends[k + 1])) for k in range(CELLS + 1)]
    row_d = d_ref[pl.ds(me, 1), :]
    row_wall = wall_ref[pl.ds(me, 1), :]
    row_low = (row_wall & 1).astype(F32) * across(floor_scale[0:1])
    row_high = (row_wall >> 1).astype(F32) * across(roof_scale[0:1])
    faces[0] = jnp.where(block_id == 0, row_low, faces[0])
    faces[CELLS] = jnp.where(block_id == BLOCKS - 1, row_high, faces[CELLS])
    dd = jnp.broadcast_to(row_d, (BLOCKS, LANES))
    w = None
    q = dd * faces[0]
    first_edge = q
    alpha = None
    for k in range(INNER):
        low, high = dd * faces[k], dd * faces[k + 1]
        pivot = across(heights[k]) + (low + high)
        if k:
            pivot = pivot - low * w
        inv = inverse(pivot)
        w = high * inv
        gain = q * q * inv
        alpha = gain if alpha is None else alpha + gain
        q = q * w
    high = dd * faces[INNER]
    last_edge = dd * faces[CELLS]
    own_diagonal = across(heights[INNER]) + (high + last_edge) - high * w
    for a, b in tiles_of():
        for half in (0, 4):
            at = pl.ds(a * 64 + b + half, 8, stride=8)
            al_ref[at, :] = part(alpha, a, b)
            be_ref[at, :] = part(q, a, b)
            dh_ref[at, :] = part(own_diagonal, a, b)
    for b in range(TILES):
        for half in (0, 4):
            z_ref[pl.ds(b + half, 8, stride=8), :] = part(first_edge, 0, b)
            y_ref[pl.ds(b + half, 8, stride=8), :] = part(last_edge, BLOCKS // 8 - 1, b)
    floor_edge = z_ref[0:8]
    roof_edge = y_ref[56:64]
    zero = jnp.zeros((8, 128), F32)
    al_ref[256:264] = zero
    be_ref[256:264] = zero
    upper_half = lax.broadcasted_iota(jnp.int32, (8, 128), 0) < 4

    def rows8(at):
        return pl.ds(pl.multiple_of(at * 8, 8), 8)

    def factor(j, carry):
        g, z = carry
        beta = be_ref[rows8(j)]
        pivot = dh_ref[rows8(j)] - al_ref[rows8(j + 1)] - beta * g
        im = inverse(pivot)
        a = beta * im
        g = be_ref[rows8(j + 1)] * im
        z = a * z
        im_ref[rows8(j)] = im
        a_ref[rows8(j)] = a
        g_ref[rows8(j)] = g
        z_ref[rows8(j)] = z
        return g, z

    one = jnp.ones((8, 128), F32)
    _, z = lax.fori_loop(0, BLOCKS, factor, (zero, one))
    t = z + roof_edge * im_ref[(BLOCKS - 1) * 8:BLOCKS * 8]
    t_ref[(BLOCKS - 1) * 8:BLOCKS * 8] = t
    roof_t = t

    def unit_back(step, t):
        j = BLOCKS - 2 - step
        now = z_ref[rows8(j)] + g_ref[rows8(j)] * t
        t_ref[rows8(j)] = now
        tsend[rows8(j + 1)] = jnp.where(upper_half, now, t)
        return now

    t = lax.fori_loop(0, BLOCKS - 1, unit_back, t)
    tsend[0:8] = jnp.where(upper_half, one, t)
    send_all(tsend, tbuf_ref, 8, 1)
    height_sum = heights[0]
    for k in range(1, CELLS):
        height_sum = height_sum + heights[k]
    column = jnp.sum(height_sum, axis=0, keepdims=True)
    weight = column - (floor_edge - al_ref[0:8] - be_ref[0:8] * t) - roof_edge * (1.0 - roof_t)

    frecv[BLOCKS * MSG:(BLOCKS + 1) * MSG] = jnp.zeros((MSG, 128), F32)
    wait_all(frecv, MSG, recv_sem.at[0])

    def rowsm(j, group):
        return pl.ds(pl.multiple_of(j * MSG + group * 8, 8), 8)

    def solve_down(j, carry):
        z01, z2, flow = carry
        rho01 = frecv[rowsm(j, 0)] + frecv[rowsm(j + 1, 1)]
        rho2 = frecv[rowsm(j, 2)] + pltpu.roll(frecv[rowsm(j + 1, 2)], 4, 0)
        im, a = im_ref[rows8(j)], a_ref[rows8(j)]
        flow = flow + rho01 * t_ref[rows8(j)]
        z01 = rho01 * im + a * z01
        z2 = rho2 * im + a * z2
        z_ref[rows8(j)] = z01
        y_ref[rows8(j)] = z2
        return z01, z2, flow

    _, _, flow = lax.fori_loop(0, BLOCKS, solve_down, (zero, zero, frecv[8:16]))
    local = local + pltpu.roll(local, 4, 0)
    both = jnp.where(upper_half, local - flow, weight)
    flow_out[0:1] = jnp.sum(jnp.where(upper_half, both, 0.0), axis=0, keepdims=True)[None]
    flow_out[1:2] = jnp.sum(jnp.where(upper_half, 0.0, both), axis=0, keepdims=True)[None]

    def send_flow(step, carry):
        peer = lax.rem(me + step, BLOCKS)
        pltpu.make_async_remote_copy(
            src_ref=flow_out, dst_ref=flow_in.at[pl.ds(me * 2, 2)],
            send_sem=send_sem.at[2], recv_sem=recv_sem.at[2],
            device_id={"gz": peer}, device_id_type=MESH).start()
        return carry

    lax.fori_loop(1, BLOCKS, send_flow, 0)
    flow_in[pl.ds(me * 2, 2)] = flow_out[...]

    def solve_up(step, carry):
        s01, s2 = carry
        j = BLOCKS - 1 - step
        g = g_ref[rows8(j)]
        now01 = z_ref[rows8(j)] + g * s01
        now2 = y_ref[rows8(j)] + g * s2
        rsend[rowsm(j, 1)] = now01
        rsend[rowsm(j + 1, 0)] = now01
        rsend[rowsm(j + 1, 2)] = jnp.where(upper_half, now2, pltpu.roll(s2, 4, 0))
        return now01, now2

    _, s2 = lax.fori_loop(0, BLOCKS, solve_up, (zero, zero))
    rsend[0:8] = zero
    rsend[16:24] = jnp.where(upper_half, 0.0, pltpu.roll(s2, 4, 0))
    send_all(rsend, ret_ref, MSG, 3)

    span = flow_in.at[pl.ds(0, (BLOCKS - 1) * 2)]
    pltpu.make_async_copy(span, span, recv_sem.at[2]).wait()

    def add_up(j, carry):
        return carry[0] + flow_in[j * 2], carry[1] + flow_in[j * 2 + 1]

    line = jnp.zeros((1, 128), F32)
    flow, weight = lax.fori_loop(0, BLOCKS, add_up, (line, line))
    plane_out[0] = flow
    plane_out[1] = weight

    def send_plane(step, carry):
        peer = lax.rem(plane + step, PLANES)
        pltpu.make_async_remote_copy(
            src_ref=plane_out, dst_ref=plane_in.at[pl.ds(plane * 2, 2)],
            send_sem=send_sem.at[4], recv_sem=recv_sem.at[4],
            device_id={"gy": peer}, device_id_type=MESH).start()
        return carry

    lax.fori_loop(1, PLANES, send_plane, 0)
    plane_in[pl.ds(plane * 2, 2)] = plane_out[...]
    span = plane_in.at[pl.ds(0, (PLANES - 1) * 2)]
    pltpu.make_async_copy(span, span, recv_sem.at[4]).wait()
    flow, weight = line, line
    for j in range(PLANES):
        flow = flow + plane_in[2 * j]
        weight = weight + plane_in[2 * j + 1]
    flow = jnp.sum(jnp.broadcast_to(flow, (8, 128)), axis=1, keepdims=True)
    weight = jnp.sum(jnp.broadcast_to(weight, (8, 128)), axis=1, keepdims=True)
    lines = float(PLANES * ROWS * LANES)
    volume = jnp.broadcast_to(column, (8, 128)) * lines
    fix_ref[...] = (bulk_ref[0] * volume - jnp.broadcast_to(flow, (8, 128))) / jnp.broadcast_to(weight, (8, 128))

    wait_all(tbuf_ref, 8, recv_sem.at[1])
    wait_all(ret_ref, MSG, recv_sem.at[3])
    wait_all(fsend, MSG, send_sem.at[0])
    wait_all(tsend, 8, send_sem.at[1])
    wait_all(rsend, MSG, send_sem.at[3])
    span = flow_in.at[pl.ds(0, (BLOCKS - 1) * 2)]
    pltpu.make_async_copy(span, span, send_sem.at[2]).wait()
    span = plane_in.at[pl.ds(0, (PLANES - 1) * 2)]
    pltpu.make_async_copy(span, span, send_sem.at[4]).wait()


def finish_kernel(p_ref, l_ref, r_ref, ret_ref, tbuf_ref, fix_ref, out_hbm, out_ref, sem):
    def unpack(ref, row, step):
        bands = []
        for a in range(ROWS // 8):
            bands.append(jnp.concatenate(
                [ref[pl.ds(a * 8 * step + row + b, 8, stride=step), :] for b in range(TILES)], axis=1))
        return jnp.concatenate(bands, axis=0)

    copies = []
    for c in (1, 2, 0):
        before = unpack(ret_ref, c * 4 if c < 2 else 16, MSG)
        own = unpack(ret_ref, 8 + c * 4 if c < 2 else 20, MSG)
        fix = 0.0
        if c == 0:
            fix = wide(fix_ref[...])
            before = before - fix * unpack(tbuf_ref, 0, 8)
            own = own - fix * unpack(tbuf_ref, 4, 8)
        for k in range(CELLS):
            if k < INNER:
                value = p_ref[c, k] + l_ref[k] * before + r_ref[k] * own
            else:
                value = own
            out_ref[c, k] = value + fix if c == 0 else value
            if k % 4 == 3:
                span = pl.ds(k - 3, 4)
                copy = pltpu.make_async_copy(out_ref.at[c, span], out_hbm.at[c, span], sem.at[c, k // 4])
                copy.start()
                copies.append(copy)
    for copy in copies:
        copy.wait()


def shards(velocity, diffusion, wall_types, stretch_index, bulk_target):
    hbm = pl.BlockSpec(memory_space=pltpu.HBM)
    vmem = pl.BlockSpec(memory_space=pltpu.VMEM)
    plane = (ROWS, LANES)
    mids = pl.pallas_call(
        reduce_kernel,
        name="reduce_and_solve",
        out_shape=[
            pltpu.VMEM((3, INNER) + plane, F32),
            pltpu.VMEM((INNER,) + plane, F32),
            pltpu.VMEM((INNER,) + plane, F32),
            pltpu.VMEM((BLOCKS * MSG, 128), F32),
            pltpu.VMEM((BLOCKS * 8, 128), F32),
            pltpu.VMEM((8, 128), F32),
        ],
        in_specs=[hbm] * 5,
        out_specs=[vmem] * 6,
        scratch_shapes=[
            pltpu.VMEM((3, CELLS) + plane, F32),
            pltpu.VMEM(plane, F32),
            pltpu.VMEM(plane, jnp.int32),
            pltpu.SMEM((BLOCKS * CELLS,), jnp.int32),
            pltpu.SMEM((1,), F32),
            pltpu.VMEM((INNER,) + plane, F32),
            pltpu.VMEM((INNER,) + plane, F32),
            pltpu.VMEM((CELLS, BLOCKS, 128), F32),
            pltpu.VMEM((BLOCKS * MSG, 128), F32),
            pltpu.VMEM(((BLOCKS + 1) * MSG, 128), F32),
            *[pltpu.VMEM(((BLOCKS + 1) * 8, 128), F32)] * 9,
            pltpu.VMEM((BLOCKS * 8, 128), F32),
            pltpu.VMEM(((BLOCKS + 1) * MSG, 128), F32),
            pltpu.VMEM((2, 1, 128), F32),
            pltpu.VMEM((BLOCKS * 2, 1, 128), F32),
            pltpu.VMEM((2, 1, 128), F32),
            pltpu.VMEM((PLANES * 2, 1, 128), F32),
            pltpu.SemaphoreType.DMA((4,)),
            pltpu.SemaphoreType.DMA((3,)),
            pltpu.SemaphoreType.DMA((5,)),
            pltpu.SemaphoreType.DMA((5,)),
        ],
        compiler_params=pltpu.CompilerParams(
            collective_id=0, has_side_effects=True, vmem_limit_bytes=24 * 2**20),
    )(*[pltpu.with_memory_space_constraint(x, pltpu.HBM)
        for x in (velocity, diffusion, wall_types, stretch_index)], bulk_target)
    return pl.pallas_call(
        finish_kernel,
        name="finish",
        out_shape=jax.ShapeDtypeStruct((3, CELLS) + plane, F32),
        in_specs=[vmem] * 6,
        out_specs=hbm,
        scratch_shapes=[pltpu.VMEM((3, CELLS) + plane, F32), pltpu.SemaphoreType.DMA((3, 4))],
        compiler_params=pltpu.CompilerParams(vmem_limit_bytes=24 * 2**20),
    )(*mids)


def solution(mesh):
    return jax.shard_map(
        shards,
        mesh=mesh,
        in_specs=(P(None, "gz", "gy", None), P("gy", None), P("gy", None), P(), P()),
        out_specs=P(None, "gz", "gy", None),
        check_vma=False,
    )
```

time: 550 us -> 31.4 us (0.06); the launches traced: 543 us -> 31.3 us
  other arithmetic: 276 us -> 0 us
  local copies, waits for them, and re-layouts: 88.7 us -> 0 us
  waiting for transfers between devices: 79.5 us -> 0 us
  blocking collectives: 75.8 us -> 0 us
  Pallas kernels: 0 us -> 30.6 us
  between operations: 17.5 us -> 0.66 us
    dynamic_update_slice x141 -> x0, other arithmetic: 250 us -> none  [scan_thomas(): lax.scan(forward, zero_state, (lower_band, diagonal, upper_band, rhs_rows))]
    psum x1 -> x0, blocking collectives: 75.8 us -> none  [corrected(): lax.psum((partial_flow, partial_weight), ('gz', 'gy'))]
    all_gather x1 -> x0, waiting for transfers between devices: 74.6 us -> none  [shards(): gathered = lax.all_gather(reduced[None], 'gz', axis=0, tiled=True)]
    mul x49 -> x0, local copies, waits for them, and re-layouts: 51.6 us -> none  [the longest x47 48.9 us: backward(): current = solved_row - factor[None] * following]
    pallas_call x0 -> x2, Pallas kernels: none -> 30.6 us  [the longest x1 28.8 us: shards(): pl.pallas_call(reduce_kernel, name='reduce_and_solve', out_shape=[pltpu.V...]
    another operation x4 -> x0, local copies, waits for them, and re-layouts: 15.4 us -> none
    slice x4 -> x0, local copies, waits for them, and re-layouts: 11.2 us -> none  [the longest x1 8.54 us: shards(): gathered[:, 3:]]
    mul x6 -> x0, other arithmetic: 8.96 us -> none  [the longest x1 2.55 us: shards(): heights[:, None, None, None] * jnp.moveaxis(velocity, 0, 1)]
  transfers between devices with their start and end apart: 2 -> 0, of which waited for: 2 -> 0; matrix products, arithmetic and copies ran while one was open for 0% -> 0% of each run, Pallas kernels for 0% -> 0%
where the time goes in v1:
time: 31.4 us; the launch traced here: 31.3 us
  Pallas kernels  30.6 us (97%)
  between operations  0.66 us (2%)
    pallas_call x1, Pallas kernels, shards(): pl.pallas_call(reduce_kernel, name='reduce_and_solve', out_shape=[pltpu.V...  28.8 us
    pallas_call x1, Pallas kernels, shards(): pl.pallas_call(finish_kernel, name='finish', out_shape=jax.ShapeDtypeStru...  1.81 us

profile of v1, /device:TPU:1, one launch (start us, length us, event | category | flops | bytes accessed | tf_op | source)
XLA Modules:
  0.0 31.3 jit_solution(13812174468607147781)
XLA Ops:
  0.7 28.8 %reduce_and_solve.1 = (f32[3,15,32,512]{3,2,1,0:T(8,128)S(1)}, f32[15,32,512]{2,1,0:T(8,128)S(1)}, f32[15,32,512]{2,1,0:T(8,128)S(1)}, f32[768,128]{1,0:T(8,128)...) custom-call(f32[3,16,32,512]{3,2,1,0:T(8,128)} %velocity.1, f32[32,512]{1,0:T(8,128)} %diffusion.1, s32[32,512]{1,0:T(8,128)} %walls.1, ...), custom_call_target="tpu_custom_call" | custom-call | tf_op jit(solution)/shard_map/reduce_and_solve/pallas_call | solution.py:395
  29.5 1.8 %finish.1 = f32[3,16,32,512]{3,2,1,0:T(8,128)} custom-call(f32[3,15,32,512]{3,2,1,0:T(8,128)S(1)} %get-tuple-element.11.p_ref, f32[15,32,512]{2,1,0:T(8,128)S(1)} %get-tuple-element.12.l_ref, f32[15,32,512]{2,1,0:T(8,128)S(1)} %get-tuple-element.13.r_ref, f32[768,128]{1,0:T(8,128)S(1)} %get-tuple-element.14.ret_ref, ...), custom_call_target="tpu_custom_call" | custom-call | tf_op jit(solution)/shard_map/finish/pallas_call | solution.py:435

commit v2 on v1

v2 whole, which is shorter than its diff:
```python
import jax
import jax.numpy as jnp
from jax import lax
from jax.experimental import pallas as pl
from jax.experimental.pallas import tpu as pltpu
from jax.sharding import PartitionSpec as P

MESH = pl.DeviceIdType.MESH
F32 = jnp.float32
BLOCKS = 32
PLANES = 8
CELLS = 16
INNER = CELLS - 1
ROWS = 32
LANES = 512
TILES = LANES // 128
MSG = 8
GROUP = 8


def inverse(x):
    guess = pl.reciprocal(x, approx=True)
    return guess * (2.0 - x * guess)


def wide(tile):
    row = jnp.concatenate([tile] * TILES, axis=1)
    return jnp.concatenate([row] * (ROWS // 8), axis=0)


def across(column):
    return jnp.concatenate([column] * TILES, axis=1)


def tiles_of():
    return [(a, b) for a in range(ROWS // 8) for b in range(TILES)]


def part(x, a, b):
    return x[a * 8:(a + 1) * 8, b * 128:(b + 1) * 128]


def reduce_kernel(velocity, diffusion, walls, stretch, bulk,
                  p_ref, l_ref, r_ref, ret_ref, tbuf_ref, fix_ref,
                  v_ref, d_ref, wall_ref, stretch_ref, bulk_ref, w_ref, inv_ref, hb_ref,
                  fsend, frecv, al_ref, be_ref, dh_ref, im_ref, a_ref, g_ref, t_ref, z_ref, y_ref,
                  tsend, rsend, flow_out, flow_in, plane_out, plane_in,
                  load_sem, v_sem, send_sem, recv_sem):
    me = lax.axis_index("gz")
    plane = lax.axis_index("gy")

    def load(src, dst, sem):
        copy = pltpu.make_async_copy(src, dst, sem)
        copy.start()
        return copy

    stretch_load = load(stretch, stretch_ref, load_sem.at[0])
    d_load = load(diffusion, d_ref, load_sem.at[2])
    wall_load = load(walls, wall_ref, load_sem.at[3])
    v_loads = [load(velocity.at[c], v_ref.at[c], v_sem.at[c]) for c in range(3)]
    bulk_load = load(bulk, bulk_ref, load_sem.at[1])

    barrier = pltpu.get_barrier_semaphore()

    def greet(step, carry):
        pl.semaphore_signal(barrier, 1, device_id={"gz": lax.rem(me + step, BLOCKS)}, device_id_type=MESH)
        return carry

    def greet_plane(step, carry):
        pl.semaphore_signal(barrier, 1, device_id={"gy": lax.rem(plane + step, PLANES)}, device_id_type=MESH)
        return carry

    lax.fori_loop(1, BLOCKS, greet, 0)
    lax.fori_loop(1, PLANES, greet_plane, 0)

    stretch_load.wait()

    def height(cell):
        return 0.5 + 0.25 * stretch_ref[cell].astype(F32)

    first = me * CELLS
    h = [height(first + k) for k in range(CELLS)]
    below = height(jnp.maximum(first - 1, 0))

    def face(one, other):
        return 2.0 * inverse(jnp.full((8, 128), one + other, F32))

    ends = [below] + h
    f = [wide(face(ends[k], ends[k + 1])) for k in range(CELLS)]
    floor_scale = 2.0 * inverse(jnp.full((8, 128), height(0), F32))
    roof_scale = 2.0 * inverse(jnp.full((8, 128), height(BLOCKS * CELLS - 1), F32))
    d_load.wait()
    wall_load.wait()
    d = d_ref[...]
    lower_wall = (wall_ref[...] & 1).astype(F32) * wide(floor_scale)
    edge_low = d * jnp.where(me == 0, lower_wall, f[0])

    w = None
    low = edge_low
    for k in range(INNER):
        high = d * f[k + 1]
        pivot = h[k] + (low + high)
        if k:
            pivot = pivot - low * w
        inv = inverse(pivot)
        w = high * inv
        low = high
        inv_ref[k] = inv
        w_ref[k] = w
    edge_high = low

    def send_all(src, dst, which):
        x, y, core = me // 8, lax.rem(me // 2, 4), lax.rem(me, 2)

        def offset(place):
            return jnp.where(place == 0, 2, jnp.where(place == 1, 1, jnp.where(place == 2, 3, 0)))

        def one(step, carry):
            to_x = lax.rem(x + offset(step // 8), 4)
            to_y = lax.rem(y + offset(lax.rem(step // 2, 4)), 4)
            to_core = lax.rem(core + 1 + lax.rem(step, 2), 2)
            peer = to_x * 8 + to_y * 2 + to_core
            pltpu.make_async_remote_copy(
                src_ref=src.at[pl.ds(pl.multiple_of(peer * MSG, MSG), MSG)],
                dst_ref=dst.at[pl.ds(pl.multiple_of(me * MSG, MSG), MSG)],
                send_sem=send_sem.at[which], recv_sem=recv_sem.at[which],
                device_id={"gz": peer}, device_id_type=MESH).start()
            return carry

        lax.fori_loop(0, BLOCKS - 1, one, 0)
        mine = pl.ds(pl.multiple_of(me * MSG, MSG), MSG)
        dst[mine] = src[mine]

    def wait_all(ref, rows, sem):
        span = ref.at[pl.ds(0, (BLOCKS - 1) * rows)]
        pltpu.make_async_copy(span, span, sem).wait()

    total = jnp.zeros((ROWS, LANES), F32)
    for c in range(3):
        v_loads[c].wait()
        y = None
        for k in range(INNER):
            rhs = h[k] * v_ref[c, k]
            if c == 0:
                total = total + rhs
            y = rhs if k == 0 else rhs + w_ref[k - 1] * y
            p_ref[c, k] = y
        x = inv_ref[INNER - 1] * y
        p_ref[c, INNER - 1] = x
        own = h[INNER] * v_ref[c, INNER]
        if c == 0:
            total = total + own
        own = own + edge_high * x
        for k in range(INNER - 2, -1, -1):
            x = inv_ref[k] * p_ref[c, k] + w_ref[k] * x
            p_ref[c, k] = x
        other = edge_low * x
        for a, b in tiles_of():
            at = a * 8 * MSG + b
            fsend[c, pl.ds(at, 8, stride=MSG), :] = part(own, a, b)
            fsend[c, pl.ds(at + 4, 8, stride=MSG), :] = part(other, a, b)
        if c == 0:
            pl.semaphore_wait(barrier, BLOCKS - 1 + PLANES - 1)
        send_all(fsend.at[c], frecv.at[c], c)
    local = jnp.zeros((8, 128), F32)
    for a, b in tiles_of():
        local = local + part(total, a, b)

    def table_row(block, carry):
        for k in range(CELLS):
            hb_ref[k, pl.ds(block, 1), :] = jnp.full((1, 128), height(block * CELLS + k), F32)
        return carry

    lax.fori_loop(0, BLOCKS, table_row, 0)
    block_id = lax.broadcasted_iota(jnp.int32, (BLOCKS, LANES), 0)
    heights = [hb_ref[k] for k in range(CELLS)]
    before = pltpu.roll(heights[INNER], 1, 0)
    after = pltpu.roll(heights[0], BLOCKS - 1, 0)
    ends = [before] + heights + [after]
    faces = [across(2.0 * inverse(ends[k] + ends[k + 1])) for k in range(CELLS + 1)]
    row_d = d_ref[pl.ds(me, 1), :]
    row_wall = wall_ref[pl.ds(me, 1), :]
    row_low = (row_wall & 1).astype(F32) * across(floor_scale[0:1])
    row_high = (row_wall >> 1).astype(F32) * across(roof_scale[0:1])
    faces[0] = jnp.where(block_id == 0, row_low, faces[0])
    faces[CELLS] = jnp.where(block_id == BLOCKS - 1, row_high, faces[CELLS])
    dd = jnp.broadcast_to(row_d, (BLOCKS, LANES))
    w = None
    q = dd * faces[0]
    first_edge = q
    alpha = None
    for k in range(INNER):
        low, high = dd * faces[k], dd * faces[k + 1]
        pivot = across(heights[k]) + (low + high)
        if k:
            pivot = pivot - low * w
        inv = inverse(pivot)
        w = high * inv
        gain = q * q * inv
        alpha = gain if alpha is None else alpha + gain
        q = q * w
    high = dd * faces[INNER]
    last_edge = dd * faces[CELLS]
    own_diagonal = across(heights[INNER]) + (high + last_edge) - high * w
    for a, b in tiles_of():
        for half in (0, 4):
            at = pl.ds(a * 64 + b + half, 8, stride=8)
            al_ref[at, :] = part(alpha, a, b)
            be_ref[at, :] = part(q, a, b)
            dh_ref[at, :] = part(own_diagonal, a, b)
    for b in range(TILES):
        for half in (0, 4):
            z_ref[pl.ds(b + half, 8, stride=8), :] = part(first_edge, 0, b)
            y_ref[pl.ds(b + half, 8, stride=8), :] = part(last_edge, BLOCKS // 8 - 1, b)
    floor_edge = z_ref[0:8]
    roof_edge = y_ref[56:64]
    zero = jnp.zeros((8, 128), F32)
    one = jnp.ones((8, 128), F32)
    al_ref[256:264] = zero
    be_ref[256:264] = zero
    upper_half = lax.broadcasted_iota(jnp.int32, (8, 128), 0) < 4

    def rows8(at):
        return pl.ds(pl.multiple_of(at * 8, 8), 8)

    def sweep(step, carry, backward=False):
        def group(at, carry):
            for u in range(GROUP):
                j = at * GROUP + u
                carry = step(BLOCKS - 1 - j if backward else j, carry)
            return carry
        return lax.fori_loop(0, BLOCKS // GROUP, group, carry)

    def factor(j, carry):
        g, z = carry
        beta = be_ref[rows8(j)]
        pivot = dh_ref[rows8(j)] - al_ref[rows8(j + 1)] - beta * g
        im = inverse(pivot)
        a = beta * im
        g = be_ref[rows8(j + 1)] * im
        z = a * z
        im_ref[rows8(j)] = im
        a_ref[rows8(j)] = a
        g_ref[rows8(j)] = g
        z_ref[rows8(j)] = z
        return g, z

    sweep(factor, (zero, one))
    last = pl.ds((BLOCKS - 1) * 8, 8)
    z_ref[last] = z_ref[last] + roof_edge * im_ref[last]

    def unit_back(j, t):
        now = z_ref[rows8(j)] + g_ref[rows8(j)] * t
        t_ref[rows8(j)] = now
        tsend[rows8(j + 1)] = jnp.where(upper_half, now, t)
        return now

    t = sweep(unit_back, zero, backward=True)
    tsend[0:8] = jnp.where(upper_half, one, t)
    send_all(tsend, tbuf_ref, 6)
    height_sum = heights[0]
    for k in range(1, CELLS):
        height_sum = height_sum + heights[k]
    column = jnp.sum(height_sum, axis=0, keepdims=True)
    weight = column - (floor_edge - al_ref[0:8] - be_ref[0:8] * t) - roof_edge * (1.0 - t_ref[last])

    left = edge_low
    for k in range(INNER):
        l_ref[k] = left * inv_ref[k]
        left = left * w_ref[k]
    left, right = l_ref[INNER - 1], w_ref[INNER - 1]
    r_ref[INNER - 1] = right
    for k in range(INNER - 2, -1, -1):
        w = w_ref[k]
        left = l_ref[k] + w * left
        right = w * right
        l_ref[k] = left
        r_ref[k] = right

    def solve(c):
        frecv[c, pl.ds(BLOCKS * MSG, MSG)] = zero
        wait_all(frecv.at[c], MSG, recv_sem.at[c])

        def down(j, carry):
            z, flow = carry
            rho = frecv[c, rows8(j)] + pltpu.roll(frecv[c, rows8(j + 1)], 4, 0)
            if c == 0:
                flow = flow + rho * t_ref[rows8(j)]
            z = rho * im_ref[rows8(j)] + a_ref[rows8(j)] * z
            z_ref[rows8(j)] = z
            return z, flow

        _, flow = sweep(down, (zero, pltpu.roll(frecv[c, 0:8], 4, 0)))
        if c == 0:
            sums = local + pltpu.roll(local, 4, 0)
            flow_out[0] = jnp.sum(jnp.where(upper_half, sums - flow, 0.0), axis=0, keepdims=True)
            flow_out[1] = jnp.sum(jnp.where(upper_half, weight, 0.0), axis=0, keepdims=True)

            def send_flow(step, carry):
                pltpu.make_async_remote_copy(
                    src_ref=flow_out, dst_ref=flow_in.at[pl.ds(me * 2, 2)],
                    send_sem=send_sem.at[7], recv_sem=recv_sem.at[7],
                    device_id={"gz": lax.rem(me + step, BLOCKS)}, device_id_type=MESH).start()
                return carry

            lax.fori_loop(1, BLOCKS, send_flow, 0)
            flow_in[pl.ds(me * 2, 2)] = flow_out[...]

        def up(j, s):
            now = z_ref[rows8(j)] + g_ref[rows8(j)] * s
            rsend[c, rows8(j + 1)] = jnp.where(upper_half, now, pltpu.roll(s, 4, 0))
            return now

        s = sweep(up, zero, backward=True)
        rsend[c, 0:8] = jnp.where(upper_half, 0.0, pltpu.roll(s, 4, 0))
        send_all(rsend.at[c], ret_ref.at[c], 3 + c)

    for c in range(3):
        solve(c)

    wait_all(flow_in, 2, recv_sem.at[7])

    def add_up(j, carry):
        return carry[0] + flow_in[j * 2], carry[1] + flow_in[j * 2 + 1]

    line = jnp.zeros((1, 128), F32)
    flow, weight = lax.fori_loop(0, BLOCKS, add_up, (line, line))
    plane_out[0] = flow
    plane_out[1] = weight

    def send_plane(step, carry):
        peer = lax.rem(plane + step, PLANES)
        pltpu.make_async_remote_copy(
            src_ref=plane_out, dst_ref=plane_in.at[pl.ds(plane * 2, 2)],
            send_sem=send_sem.at[8], recv_sem=recv_sem.at[8],
            device_id={"gy": peer}, device_id_type=MESH).start()
        return carry

    lax.fori_loop(1, PLANES, send_plane, 0)
    plane_in[pl.ds(plane * 2, 2)] = plane_out[...]

    wait_all(ret_ref.at[1], MSG, recv_sem.at[4])
    before, own = unpack(ret_ref.at[1], 0), unpack(ret_ref.at[1], 4)
    for k in range(INNER):
        p_ref[1, k] = p_ref[1, k] + l_ref[k] * before + r_ref[k] * own
    p_ref[1, INNER] = own

    bulk_load.wait()
    span = plane_in.at[pl.ds(0, (PLANES - 1) * 2)]
    pltpu.make_async_copy(span, span, recv_sem.at[8]).wait()
    flow, weight = line, line
    for j in range(PLANES):
        flow = flow + plane_in[2 * j]
        weight = weight + plane_in[2 * j + 1]
    flow = jnp.sum(jnp.broadcast_to(flow, (8, 128)), axis=1, keepdims=True)
    weight = jnp.sum(jnp.broadcast_to(weight, (8, 128)), axis=1, keepdims=True)
    lines = float(PLANES * ROWS * LANES)
    volume = jnp.broadcast_to(column, (8, 128)) * lines
    fix_ref[...] = (bulk_ref[0] * volume - jnp.broadcast_to(flow, (8, 128))) / jnp.broadcast_to(weight, (8, 128))

    for c in range(3):
        wait_all(fsend.at[c], MSG, send_sem.at[c])
        wait_all(rsend.at[c], MSG, send_sem.at[3 + c])
    wait_all(tsend, MSG, send_sem.at[6])
    wait_all(flow_in, 2, send_sem.at[7])
    span = plane_in.at[pl.ds(0, (PLANES - 1) * 2)]
    pltpu.make_async_copy(span, span, send_sem.at[8]).wait()
    wait_all(tbuf_ref, MSG, recv_sem.at[6])
    wait_all(ret_ref.at[0], MSG, recv_sem.at[3])
    wait_all(ret_ref.at[2], MSG, recv_sem.at[5])


def unpack(ref, row):
    bands = []
    for a in range(ROWS // 8):
        bands.append(jnp.concatenate(
            [ref[pl.ds(a * 8 * MSG + row + b, 8, stride=MSG), :] for b in range(TILES)], axis=1))
    return jnp.concatenate(bands, axis=0)


def finish_kernel(p_ref, l_ref, r_ref, ret_ref, tbuf_ref, fix_ref, out_hbm, out_ref, sem):
    copies = []

    def write(src, c, start, count):
        copy = pltpu.make_async_copy(
            src.at[c, pl.ds(start, count)], out_hbm.at[c, pl.ds(start, count)], sem.at[c, start // 4])
        copy.start()
        copies.append(copy)

    for start in range(0, CELLS, 4):
        write(p_ref, 1, start, 4)
    for c in (2, 0):
        before, own = unpack(ret_ref.at[c], 0), unpack(ret_ref.at[c], 4)
        if c == 0:
            fix = wide(fix_ref[...])
            before = before - fix * unpack(tbuf_ref, 0)
            own = own - fix * unpack(tbuf_ref, 4)
        for k in range(CELLS):
            if k < INNER:
                value = p_ref[c, k] + l_ref[k] * before + r_ref[k] * own
            else:
                value = own
            out_ref[c, k] = value + fix if c == 0 else value
            if k % 4 == 3:
                write(out_ref, c, k - 3, 4)
    for copy in copies:
        copy.wait()


def shards(velocity, diffusion, wall_types, stretch_index, bulk_target):
    hbm = pl.BlockSpec(memory_space=pltpu.HBM)
    vmem = pl.BlockSpec(memory_space=pltpu.VMEM)
    plane = (ROWS, LANES)
    mids = pl.pallas_call(
        reduce_kernel,
        name="reduce_and_solve",
        out_shape=[
            pltpu.VMEM((3, CELLS) + plane, F32),
            pltpu.VMEM((INNER,) + plane, F32),
            pltpu.VMEM((INNER,) + plane, F32),
            pltpu.VMEM((3, BLOCKS * MSG, 128), F32),
            pltpu.VMEM((BLOCKS * MSG, 128), F32),
            pltpu.VMEM((8, 128), F32),
        ],
        in_specs=[hbm] * 5,
        out_specs=[vmem] * 6,
        scratch_shapes=[
            pltpu.VMEM((3, CELLS) + plane, F32),
            pltpu.VMEM(plane, F32),
            pltpu.VMEM(plane, jnp.int32),
            pltpu.SMEM((BLOCKS * CELLS,), jnp.int32),
            pltpu.SMEM((1,), F32),
            pltpu.VMEM((INNER,) + plane, F32),
            pltpu.VMEM((INNER,) + plane, F32),
            pltpu.VMEM((CELLS, BLOCKS, 128), F32),
            pltpu.VMEM((3, BLOCKS * MSG, 128), F32),
            pltpu.VMEM((3, (BLOCKS + 1) * MSG, 128), F32),
            *[pltpu.VMEM(((BLOCKS + 1) * 8, 128), F32)] * 9,
            pltpu.VMEM(((BLOCKS + 1) * MSG, 128), F32),
            pltpu.VMEM((3, (BLOCKS + 1) * MSG, 128), F32),
            pltpu.VMEM((2, 1, 128), F32),
            pltpu.VMEM((BLOCKS * 2, 1, 128), F32),
            pltpu.VMEM((2, 1, 128), F32),
            pltpu.VMEM((PLANES * 2, 1, 128), F32),
            pltpu.SemaphoreType.DMA((4,)),
            pltpu.SemaphoreType.DMA((3,)),
            pltpu.SemaphoreType.DMA((9,)),
            pltpu.SemaphoreType.DMA((9,)),
        ],
        compiler_params=pltpu.CompilerParams(
            collective_id=0, has_side_effects=True, vmem_limit_bytes=24 * 2**20),
    )(*[pltpu.with_memory_space_constraint(x, pltpu.HBM)
        for x in (velocity, diffusion, wall_types, stretch_index)], bulk_target)
    return pl.pallas_call(
        finish_kernel,
        name="finish",
        out_shape=jax.ShapeDtypeStruct((3, CELLS) + plane, F32),
        in_specs=[vmem] * 6,
        out_specs=hbm,
        scratch_shapes=[pltpu.VMEM((3, CELLS) + plane, F32), pltpu.SemaphoreType.DMA((3, 4))],
        compiler_params=pltpu.CompilerParams(vmem_limit_bytes=24 * 2**20),
    )(*mids)


def solution(mesh):
    return jax.shard_map(
        shards,
        mesh=mesh,
        in_specs=(P(None, "gz", "gy", None), P("gy", None), P("gy", None), P(), P()),
        out_specs=P(None, "gz", "gy", None),
        check_vma=False,
    )
```

time: 31.4 us -> 28.8 us (0.917)
  Pallas kernels: 30.6 us -> 28 us
    pallas_call x1, Pallas kernels: 28.8 us -> 26.3 us  [shards(): pl.pallas_call(reduce_kernel, name='reduce_and_solve', out_shape=[pltpu.V...]
where the time goes in v2:
time: 28.8 us; the launch traced here: 28.7 us
  Pallas kernels  28 us (97%)
  between operations  0.66 us (2%)
    pallas_call x1, Pallas kernels, shards(): pl.pallas_call(reduce_kernel, name='reduce_and_solve', out_shape=[pltpu.V...  26.3 us
    pallas_call x1, Pallas kernels, shards(): pl.pallas_call(finish_kernel, name='finish', out_shape=jax.ShapeDtypeStru...  1.76 us

profile of v2, /device:TPU:1, one launch (start us, length us, event | category | flops | bytes accessed | tf_op | source)
XLA Modules:
  0.0 28.7 jit_solution(973388056147955994)
XLA Ops:
  0.7 26.3 %reduce_and_solve.1 = (f32[3,16,32,512]{3,2,1,0:T(8,128)S(1)}, f32[15,32,512]{2,1,0:T(8,128)S(1)}, f32[15,32,512]{2,1,0:T(8,128)S(1)}, f32[3,256,128]{2,1,0:T(8,...) custom-call(f32[3,16,32,512]{3,2,1,0:T(8,128)} %velocity.1, f32[32,512]{1,0:T(8,128)} %diffusion.1, ...), custom_call_target="tpu_custom_call" | custom-call | tf_op jit(solution)/shard_map/reduce_and_solve/pallas_call | solution.py:414
  26.9 1.8 %finish.1 = f32[3,16,32,512]{3,2,1,0:T(8,128)} custom-call(f32[3,16,32,512]{3,2,1,0:T(8,128)S(1)} %get-tuple-element.11.p_ref, f32[15,32,512]{2,1,0:T(8,128)S(1)} %get-tuple-element.12.l_ref, f32[15,32,512]{2,1,0:T(8,128)S(1)} %get-tuple-element.13.r_ref, f32[3,256,128]{2,1,0:T(8,128)S(1)} %get-tuple-element.14.ret_ref, ...), custom_call_target="tpu_custom_call" | custom-call | tf_op jit(solution)/shard_map/finish/pallas_call | solution.py:454

commit v3 on v2

--- a/solution.py
+++ b/solution.py
@@ -18,6 +18,9 @@
 GROUP = 8
 
 
+FAR_FIRST = sorted(range(1, BLOCKS), key=lambda i: -min(i // 8, 4 - i // 8) - min(i // 2 % 4, 4 - i // 2 % 4))
+
+
 def inverse(x):
     guess = pl.reciprocal(x, approx=True)
     return guess * (2.0 - x * guess)
@@ -41,11 +44,11 @@
 
 
 def reduce_kernel(velocity, diffusion, walls, stretch, bulk,
-                  p_ref, l_ref, r_ref, ret_ref, tbuf_ref, fix_ref,
-                  v_ref, d_ref, wall_ref, stretch_ref, bulk_ref, w_ref, inv_ref, hb_ref,
+                  p_ref, u_ref, fix_ref,
+                  l_ref, r_ref, ret_ref, tbuf_ref, v_ref, d_ref, wall_ref, stretch_ref, bulk_ref, w_ref, inv_ref, hb_ref,
                   fsend, frecv, al_ref, be_ref, dh_ref, im_ref, a_ref, g_ref, t_ref, z_ref, y_ref,
                   tsend, rsend, flow_out, flow_in, plane_out, plane_in,
-                  load_sem, v_sem, send_sem, recv_sem):
+                  load_sem, v_sem, send_sem, recv_sem, plane_sem):
     me = lax.axis_index("gz")
     plane = lax.axis_index("gy")
 
@@ -54,24 +57,23 @@
         copy.start()
         return copy
 
+    barrier = pltpu.get_barrier_semaphore()
+
+    def greet(step, carry):
+        pl.semaphore_signal(barrier, 1, device_id={"gz": lax.rem(me + step, BLOCKS)}, device_id_type=MESH)
+        return carry
+
+    def greet_plane(other, carry):
+        pl.semaphore_signal(barrier, 1, device_id={"gy": other}, device_id_type=MESH)
+        return carry
+
+    lax.fori_loop(1, BLOCKS, greet, 0)
+    lax.fori_loop(plane + 1, PLANES, greet_plane, 0)
+
     stretch_load = load(stretch, stretch_ref, load_sem.at[0])
     d_load = load(diffusion, d_ref, load_sem.at[2])
     wall_load = load(walls, wall_ref, load_sem.at[3])
-    v_loads = [load(velocity.at[c], v_ref.at[c], v_sem.at[c]) for c in range(3)]
-    bulk_load = load(bulk, bulk_ref, load_sem.at[1])
-
-    barrier = pltpu.get_barrier_semaphore()
-
-    def greet(step, carry):
-        pl.semaphore_signal(barrier, 1, device_id={"gz": lax.rem(me + step, BLOCKS)}, device_id_type=MESH)
-        return carry
-
-    def greet_plane(step, carry):
-        pl.semaphore_signal(barrier, 1, device_id={"gy": lax.rem(plane + step, PLANES)}, device_id_type=MESH)
-        return carry
-
-    lax.fori_loop(1, BLOCKS, greet, 0)
-    lax.fori_loop(1, PLANES, greet_plane, 0)
+    v_loads = [load(velocity.at[0], v_ref.at[0], v_sem.at[0])]
 
     stretch_load.wait()
 
@@ -91,6 +93,8 @@
     roof_scale = 2.0 * inverse(jnp.full((8, 128), height(BLOCKS * CELLS - 1), F32))
     d_load.wait()
     wall_load.wait()
+    v_loads += [load(velocity.at[c], v_ref.at[c], v_sem.at[c]) for c in (1, 2)]
+    bulk_load = load(bulk, bulk_ref, load_sem.at[1])
     d = d_ref[...]
     lower_wall = (wall_ref[...] & 1).astype(F32) * wide(floor_scale)
     edge_low = d * jnp.where(me == 0, lower_wall, f[0])
@@ -112,28 +116,23 @@
     def send_all(src, dst, which):
         x, y, core = me // 8, lax.rem(me // 2, 4), lax.rem(me, 2)
 
-        def offset(place):
-            return jnp.where(place == 0, 2, jnp.where(place == 1, 1, jnp.where(place == 2, 3, 0)))
-
-        def one(step, carry):
-            to_x = lax.rem(x + offset(step // 8), 4)
-            to_y = lax.rem(y + offset(lax.rem(step // 2, 4)), 4)
-            to_core = lax.rem(core + 1 + lax.rem(step, 2), 2)
-            peer = to_x * 8 + to_y * 2 + to_core
+        for step in FAR_FIRST:
+            peer = lax.rem(x + step // 8, 4) * 8 + lax.rem(y + (step // 2) % 4, 4) * 2 + (lax.rem(core + step % 2, 2))
             pltpu.make_async_remote_copy(
                 src_ref=src.at[pl.ds(pl.multiple_of(peer * MSG, MSG), MSG)],
                 dst_ref=dst.at[pl.ds(pl.multiple_of(me * MSG, MSG), MSG)],
                 send_sem=send_sem.at[which], recv_sem=recv_sem.at[which],
                 device_id={"gz": peer}, device_id_type=MESH).start()
-            return carry
-
-        lax.fori_loop(0, BLOCKS - 1, one, 0)
         mine = pl.ds(pl.multiple_of(me * MSG, MSG), MSG)
         dst[mine] = src[mine]
 
     def wait_all(ref, rows, sem):
         span = ref.at[pl.ds(0, (BLOCKS - 1) * rows)]
         pltpu.make_async_copy(span, span, sem).wait()
+
+    def answer_plane(other, carry):
+        pl.semaphore_signal(plane_sem, 1, device_id={"gy": other}, device_id_type=MESH)
+        return carry
 
     total = jnp.zeros((ROWS, LANES), F32)
     for c in range(3):
@@ -160,8 +159,10 @@
             fsend[c, pl.ds(at, 8, stride=MSG), :] = part(own, a, b)
             fsend[c, pl.ds(at + 4, 8, stride=MSG), :] = part(other, a, b)
         if c == 0:
-            pl.semaphore_wait(barrier, BLOCKS - 1 + PLANES - 1)
+            pl.semaphore_wait(barrier, BLOCKS - 1 + plane)
         send_all(fsend.at[c], frecv.at[c], c)
+        if c == 0:
+            lax.fori_loop(0, plane, answer_plane, 0)
     local = jnp.zeros((8, 128), F32)
     for a, b in tiles_of():
         local = local + part(total, a, b)
@@ -257,12 +258,52 @@
 
     t = sweep(unit_back, zero, backward=True)
     tsend[0:8] = jnp.where(upper_half, one, t)
-    send_all(tsend, tbuf_ref, 6)
     height_sum = heights[0]
     for k in range(1, CELLS):
         height_sum = height_sum + heights[k]
     column = jnp.sum(height_sum, axis=0, keepdims=True)
     weight = column - (floor_edge - al_ref[0:8] - be_ref[0:8] * t) - roof_edge * (1.0 - t_ref[last])
+
+    def solve(c):
+        frecv[c, pl.ds(BLOCKS * MSG, MSG)] = zero
+        wait_all(frecv.at[c], MSG, recv_sem.at[c])
+
+        def down(j, carry):
+            z, flow = carry
+            rho = frecv[c, rows8(j)] + pltpu.roll(frecv[c, rows8(j + 1)], 4, 0)
+            if c == 0:
+                flow = flow + rho * t_ref[rows8(j)]
+            z = rho * im_ref[rows8(j)] + a_ref[rows8(j)] * z
+            z_ref[rows8(j)] = z
+            return z, flow
+
+        _, flow = sweep(down, (zero, pltpu.roll(frecv[c, 0:8], 4, 0)))
+        if c == 0:
+            sums = local + pltpu.roll(local, 4, 0)
+            flow_out[0] = jnp.sum(jnp.where(upper_half, sums - flow, 0.0), axis=0, keepdims=True)
+            flow_out[1] = jnp.sum(jnp.where(upper_half, weight, 0.0), axis=0, keepdims=True)
+
+            def send_flow(step, carry):
+                pltpu.make_async_remote_copy(
+                    src_ref=flow_out, dst_ref=flow_in.at[pl.ds(me * 2, 2)],
+                    send_sem=send_sem.at[7], recv_sem=recv_sem.at[7],
+                    device_id={"gz": lax.rem(me + step, BLOCKS)}, device_id_type=MESH).start()
+                return carry
+
+            lax.fori_loop(1, BLOCKS, send_flow, 0)
+            flow_in[pl.ds(me * 2, 2)] = flow_out[...]
+
+        def up(j, s):
+            now = z_ref[rows8(j)] + g_ref[rows8(j)] * s
+            rsend[c, rows8(j + 1)] = jnp.where(upper_half, now, pltpu.roll(s, 4, 0))
+            return now
+
+        s = sweep(up, zero, backward=True)
+        rsend[c, 0:8] = jnp.where(upper_half, 0.0, pltpu.roll(s, 4, 0))
+        send_all(rsend.at[c], ret_ref.at[c], 3 + c)
+
+    solve(0)
+    send_all(tsend, tbuf_ref, 6)
 
     left = edge_low
     for k in range(INNER):
@@ -277,46 +318,8 @@
         l_ref[k] = left
         r_ref[k] = right
 
-    def solve(c):
-        frecv[c, pl.ds(BLOCKS * MSG, MSG)] = zero
-        wait_all(frecv.at[c], MSG, recv_sem.at[c])
-
-        def down(j, carry):
-            z, flow = carry
-            rho = frecv[c, rows8(j)] + pltpu.roll(frecv[c, rows8(j + 1)], 4, 0)
-            if c == 0:
-                flow = flow + rho * t_ref[rows8(j)]
-            z = rho * im_ref[rows8(j)] + a_ref[rows8(j)] * z
-            z_ref[rows8(j)] = z
-            return z, flow
-
-        _, flow = sweep(down, (zero, pltpu.roll(frecv[c, 0:8], 4, 0)))
-        if c == 0:
-            sums = local + pltpu.roll(local, 4, 0)
-            flow_out[0] = jnp.sum(jnp.where(upper_half, sums - flow, 0.0), axis=0, keepdims=True)
-            flow_out[1] = jnp.sum(jnp.where(upper_half, weight, 0.0), axis=0, keepdims=True)
-
-            def send_flow(step, carry):
-                pltpu.make_async_remote_copy(
-                    src_ref=flow_out, dst_ref=flow_in.at[pl.ds(me * 2, 2)],
-                    send_sem=send_sem.at[7], recv_sem=recv_sem.at[7],
-                    device_id={"gz": lax.rem(me + step, BLOCKS)}, device_id_type=MESH).start()
-                return carry
-
-            lax.fori_loop(1, BLOCKS, send_flow, 0)
-            flow_in[pl.ds(me * 2, 2)] = flow_out[...]
-
-        def up(j, s):
-            now = z_ref[rows8(j)] + g_ref[rows8(j)] * s
-            rsend[c, rows8(j + 1)] = jnp.where(upper_half, now, pltpu.roll(s, 4, 0))
-            return now
-
-        s = sweep(up, zero, backward=True)
-        rsend[c, 0:8] = jnp.where(upper_half, 0.0, pltpu.roll(s, 4, 0))
-        send_all(rsend.at[c], ret_ref.at[c], 3 + c)
-
-    for c in range(3):
-        solve(c)
+    solve(1)
+    solve(2)
 
     wait_all(flow_in, 2, recv_sem.at[7])
 
@@ -336,14 +339,36 @@
             device_id={"gy": peer}, device_id_type=MESH).start()
         return carry
 
+
+    @pl.when(plane < PLANES - 1)
+    def _():
+        pl.semaphore_wait(plane_sem, PLANES - 1 - plane)
+
     lax.fori_loop(1, PLANES, send_plane, 0)
     plane_in[pl.ds(plane * 2, 2)] = plane_out[...]
 
-    wait_all(ret_ref.at[1], MSG, recv_sem.at[4])
-    before, own = unpack(ret_ref.at[1], 0), unpack(ret_ref.at[1], 4)
+    def finish(c):
+        wait_all(ret_ref.at[c], MSG, recv_sem.at[3 + c])
+        before, own = unpack(ret_ref.at[c], 0), unpack(ret_ref.at[c], 4)
+        for k in range(INNER):
+            p_ref[c, k] = p_ref[c, k] + l_ref[k] * before + r_ref[k] * own
+        p_ref[c, INNER] = own
+
+    finish(0)
+    wait_all(tbuf_ref, MSG, recv_sem.at[6])
+    before, own = unpack(tbuf_ref, 0), unpack(tbuf_ref, 4)
     for k in range(INNER):
-        p_ref[1, k] = p_ref[1, k] + l_ref[k] * before + r_ref[k] * own
-    p_ref[1, INNER] = own
+        u_ref[k] = 1.0 - l_ref[k] * before - r_ref[k] * own
+    u_ref[INNER] = 1.0 - own
+    finish(1)
+    finish(2)
+    for c in range(3):
+        wait_all(fsend.at[c], MSG, send_sem.at[c])
+        wait_all(rsend.at[c], MSG, send_sem.at[3 + c])
+    wait_all(tsend, MSG, send_sem.at[6])
+    wait_all(flow_in, 2, send_sem.at[7])
+    span = plane_in.at[pl.ds(0, (PLANES - 1) * 2)]
+    pltpu.make_async_copy(span, span, send_sem.at[8]).wait()
 
     bulk_load.wait()
     span = plane_in.at[pl.ds(0, (PLANES - 1) * 2)]
@@ -358,17 +383,6 @@
     volume = jnp.broadcast_to(column, (8, 128)) * lines
     fix_ref[...] = (bulk_ref[0] * volume - jnp.broadcast_to(flow, (8, 128))) / jnp.broadcast_to(weight, (8, 128))
 
-    for c in range(3):
-        wait_all(fsend.at[c], MSG, send_sem.at[c])
-        wait_all(rsend.at[c], MSG, send_sem.at[3 + c])
-    wait_all(tsend, MSG, send_sem.at[6])
-    wait_all(flow_in, 2, send_sem.at[7])
-    span = plane_in.at[pl.ds(0, (PLANES - 1) * 2)]
-    pltpu.make_async_copy(span, span, send_sem.at[8]).wait()
-    wait_all(tbuf_ref, MSG, recv_sem.at[6])
-    wait_all(ret_ref.at[0], MSG, recv_sem.at[3])
-    wait_all(ret_ref.at[2], MSG, recv_sem.at[5])
-
 
 def unpack(ref, row):
     bands = []
@@ -378,31 +392,22 @@
     return jnp.concatenate(bands, axis=0)
 
 
-def finish_kernel(p_ref, l_ref, r_ref, ret_ref, tbuf_ref, fix_ref, out_hbm, out_ref, sem):
+def finish_kernel(p_ref, u_ref, fix_ref, out_hbm, out_ref, sem):
     copies = []
 
-    def write(src, c, start, count):
-        copy = pltpu.make_async_copy(
-            src.at[c, pl.ds(start, count)], out_hbm.at[c, pl.ds(start, count)], sem.at[c, start // 4])
+    def write(src, dst, start, slot):
+        copy = pltpu.make_async_copy(src.at[pl.ds(start, 4)], dst.at[pl.ds(start, 4)], sem.at[slot, start // 4])
         copy.start()
         copies.append(copy)
 
-    for start in range(0, CELLS, 4):
-        write(p_ref, 1, start, 4)
-    for c in (2, 0):
-        before, own = unpack(ret_ref.at[c], 0), unpack(ret_ref.at[c], 4)
-        if c == 0:
-            fix = wide(fix_ref[...])
-            before = before - fix * unpack(tbuf_ref, 0)
-            own = own - fix * unpack(tbuf_ref, 4)
-        for k in range(CELLS):
-            if k < INNER:
-                value = p_ref[c, k] + l_ref[k] * before + r_ref[k] * own
-            else:
-                value = own
-            out_ref[c, k] = value + fix if c == 0 else value
-            if k % 4 == 3:
-                write(out_ref, c, k - 3, 4)
+    for c in (1, 2):
+        for start in range(0, CELLS, 4):
+            write(p_ref.at[c], out_hbm.at[c], start, c)
+    fix = wide(fix_ref[...])
+    for k in range(CELLS):
+        out_ref[k] = p_ref[0, k] + fix * u_ref[k]
+        if k % 4 == 3:
+            write(out_ref, out_hbm.at[0], k - 3, 0)
     for copy in copies:
         copy.wait()
 
@@ -416,15 +421,16 @@
         name="reduce_and_solve",
         out_shape=[
             pltpu.VMEM((3, CELLS) + plane, F32),
+            pltpu.VMEM((CELLS,) + plane, F32),
+            pltpu.VMEM((8, 128), F32),
+        ],
+        in_specs=[hbm] * 5,
+        out_specs=[vmem] * 3,
+        scratch_shapes=[
             pltpu.VMEM((INNER,) + plane, F32),
             pltpu.VMEM((INNER,) + plane, F32),
             pltpu.VMEM((3, BLOCKS * MSG, 128), F32),
             pltpu.VMEM((BLOCKS * MSG, 128), F32),
-            pltpu.VMEM((8, 128), F32),
-        ],
-        in_specs=[hbm] * 5,
-        out_specs=[vmem] * 6,
-        scratch_shapes=[
             pltpu.VMEM((3, CELLS) + plane, F32),
             pltpu.VMEM(plane, F32),
             pltpu.VMEM(plane, jnp.int32),
@@ -446,6 +452,7 @@
             pltpu.SemaphoreType.DMA((3,)),
             pltpu.SemaphoreType.DMA((9,)),
             pltpu.SemaphoreType.DMA((9,)),
+            pltpu.SemaphoreType.REGULAR,
         ],
         compiler_params=pltpu.CompilerParams(
             collective_id=0, has_side_effects=True, vmem_limit_bytes=24 * 2**20),
@@ -455,9 +462,9 @@
         finish_kernel,
         name="finish",
         out_shape=jax.ShapeDtypeStruct((3, CELLS) + plane, F32),
-        in_specs=[vmem] * 6,
+        in_specs=[vmem] * 3,
         out_specs=hbm,
-        scratch_shapes=[pltpu.VMEM((3, CELLS) + plane, F32), pltpu.SemaphoreType.DMA((3, 4))],
+        scratch_shapes=[pltpu.VMEM((CELLS,) + plane, F32), pltpu.SemaphoreType.DMA((3, 4))],
         compiler_params=pltpu.CompilerParams(vmem_limit_bytes=24 * 2**20),
     )(*mids)
 

time: 28.8 us -> 27.7 us (0.962)
  Pallas kernels: 28 us -> 26.9 us
    pallas_call x1, Pallas kernels: 26.3 us -> 25.2 us  [shards(): pl.pallas_call(reduce_kernel, name='reduce_and_solve', out_shape=[pltpu.V...]
where the time goes in v3:
time: 27.7 us; the launch traced here: 27.6 us
  Pallas kernels  26.9 us (97%)
  between operations  0.66 us (2%)
    pallas_call x1, Pallas kernels, shards(): pl.pallas_call(reduce_kernel, name='reduce_and_solve', out_shape=[pltpu.V...  25.2 us
    pallas_call x1, Pallas kernels, shards(): pl.pallas_call(finish_kernel, name='finish', out_shape=jax.ShapeDtypeStru...  1.76 us

profile of v3, /device:TPU:1, one launch (start us, length us, event | category | flops | bytes accessed | tf_op | source)
XLA Modules:
  0.0 27.6 jit_solution(16005200710677389718)
XLA Ops:
  0.7 25.2 %reduce_and_solve.1 = (f32[3,16,32,512]{3,2,1,0:T(8,128)S(1)}, f32[16,32,512]{2,1,0:T(8,128)S(1)}, f32[8,128]{1,0:T(8,128)S(1)}) custom-call(f32[3,16,32,512]{3,2,1,0:T(8,128)} %velocity.1, f32[32,512]{1,0:T(8,128)} %diffusion.1, s32[32,512]{1,0:T(8,128)} %walls.1, s32[512]{0:T(512)} %stretch.1, f32[1]{0:T(128)S(6)} %copy.6.bulk), custom_call_target="tpu_custom_call" | custom-call | tf_op jit(solution)/shard_map/reduce_and_solve/pallas_call | solution.py:419
  25.9 1.8 %finish.1 = f32[3,16,32,512]{3,2,1,0:T(8,128)} custom-call(f32[3,16,32,512]{3,2,1,0:T(8,128)S(1)} %get-tuple-element.8.p_ref, f32[16,32,512]{2,1,0:T(8,128)S(1)} %get-tuple-element.9.u_ref, f32[8,128]{1,0:T(8,128)S(1)} %get-tuple-element.10.fix_ref), custom_call_target="tpu_custom_call" | custom-call | tf_op jit(solution)/shard_map/finish/pallas_call | solution.py:461

commit v4 on v3

--- a/solution.py
+++ b/solution.py
@@ -219,6 +219,7 @@
     one = jnp.ones((8, 128), F32)
     al_ref[256:264] = zero
     be_ref[256:264] = zero
+    low_lanes = lax.broadcasted_iota(jnp.int32, (8, 128), 1) < 64
     upper_half = lax.broadcasted_iota(jnp.int32, (8, 128), 0) < 4
 
     def rows8(at):
@@ -280,18 +281,21 @@
         _, flow = sweep(down, (zero, pltpu.roll(frecv[c, 0:8], 4, 0)))
         if c == 0:
             sums = local + pltpu.roll(local, 4, 0)
-            flow_out[0] = jnp.sum(jnp.where(upper_half, sums - flow, 0.0), axis=0, keepdims=True)
-            flow_out[1] = jnp.sum(jnp.where(upper_half, weight, 0.0), axis=0, keepdims=True)
+            flow = jnp.sum(jnp.where(upper_half, sums - flow, 0.0), axis=0, keepdims=True)
+            unit = jnp.sum(jnp.where(upper_half, weight, 0.0), axis=0, keepdims=True)
+            flow = flow + pltpu.roll(flow, 64, 1)
+            unit = unit + pltpu.roll(unit, 64, 1)
+            flow_out[0] = jnp.where(low_lanes[0:1], flow, unit)
 
             def send_flow(step, carry):
                 pltpu.make_async_remote_copy(
-                    src_ref=flow_out, dst_ref=flow_in.at[pl.ds(me * 2, 2)],
+                    src_ref=flow_out, dst_ref=flow_in.at[pl.ds(me, 1)],
                     send_sem=send_sem.at[7], recv_sem=recv_sem.at[7],
                     device_id={"gz": lax.rem(me + step, BLOCKS)}, device_id_type=MESH).start()
                 return carry
 
             lax.fori_loop(1, BLOCKS, send_flow, 0)
-            flow_in[pl.ds(me * 2, 2)] = flow_out[...]
+            flow_in[pl.ds(me, 1)] = flow_out[...]
 
         def up(j, s):
             now = z_ref[rows8(j)] + g_ref[rows8(j)] * s
@@ -302,8 +306,8 @@
         rsend[c, 0:8] = jnp.where(upper_half, 0.0, pltpu.roll(s, 4, 0))
         send_all(rsend.at[c], ret_ref.at[c], 3 + c)
 
+    send_all(tsend, tbuf_ref, 6)
     solve(0)
-    send_all(tsend, tbuf_ref, 6)
 
     left = edge_low
     for k in range(INNER):
@@ -321,20 +325,17 @@
     solve(1)
     solve(2)
 
-    wait_all(flow_in, 2, recv_sem.at[7])
-
-    def add_up(j, carry):
-        return carry[0] + flow_in[j * 2], carry[1] + flow_in[j * 2 + 1]
-
-    line = jnp.zeros((1, 128), F32)
-    flow, weight = lax.fori_loop(0, BLOCKS, add_up, (line, line))
-    plane_out[0] = flow
-    plane_out[1] = weight
+    wait_all(flow_in, 1, recv_sem.at[7])
+
+    parts = [flow_in[j] for j in range(BLOCKS)]
+    while len(parts) > 1:
+        parts = [parts[2 * j] + parts[2 * j + 1] for j in range(len(parts) // 2)]
+    plane_out[0] = parts[0]
 
     def send_plane(step, carry):
         peer = lax.rem(plane + step, PLANES)
         pltpu.make_async_remote_copy(
-            src_ref=plane_out, dst_ref=plane_in.at[pl.ds(plane * 2, 2)],
+            src_ref=plane_out, dst_ref=plane_in.at[pl.ds(plane, 1)],
             send_sem=send_sem.at[8], recv_sem=recv_sem.at[8],
             device_id={"gy": peer}, device_id_type=MESH).start()
         return carry
@@ -345,7 +346,7 @@
         pl.semaphore_wait(plane_sem, PLANES - 1 - plane)
 
     lax.fori_loop(1, PLANES, send_plane, 0)
-    plane_in[pl.ds(plane * 2, 2)] = plane_out[...]
+    plane_in[pl.ds(plane, 1)] = plane_out[...]
 
     def finish(c):
         wait_all(ret_ref.at[c], MSG, recv_sem.at[3 + c])
@@ -366,19 +367,19 @@
         wait_all(fsend.at[c], MSG, send_sem.at[c])
         wait_all(rsend.at[c], MSG, send_sem.at[3 + c])
     wait_all(tsend, MSG, send_sem.at[6])
-    wait_all(flow_in, 2, send_sem.at[7])
-    span = plane_in.at[pl.ds(0, (PLANES - 1) * 2)]
+    wait_all(flow_in, 1, send_sem.at[7])
+    span = plane_in.at[pl.ds(0, PLANES - 1)]
     pltpu.make_async_copy(span, span, send_sem.at[8]).wait()
 
     bulk_load.wait()
-    span = plane_in.at[pl.ds(0, (PLANES - 1) * 2)]
+    span = plane_in.at[pl.ds(0, PLANES - 1)]
     pltpu.make_async_copy(span, span, recv_sem.at[8]).wait()
-    flow, weight = line, line
-    for j in range(PLANES):
-        flow = flow + plane_in[2 * j]
-        weight = weight + plane_in[2 * j + 1]
-    flow = jnp.sum(jnp.broadcast_to(flow, (8, 128)), axis=1, keepdims=True)
-    weight = jnp.sum(jnp.broadcast_to(weight, (8, 128)), axis=1, keepdims=True)
+    parts = [plane_in[j] for j in range(PLANES)]
+    while len(parts) > 1:
+        parts = [parts[2 * j] + parts[2 * j + 1] for j in range(len(parts) // 2)]
+    sums = jnp.broadcast_to(parts[0], (8, 128))
+    flow = jnp.sum(jnp.where(low_lanes, sums, 0.0), axis=1, keepdims=True)
+    weight = jnp.sum(jnp.where(low_lanes, 0.0, sums), axis=1, keepdims=True)
     lines = float(PLANES * ROWS * LANES)
     volume = jnp.broadcast_to(column, (8, 128)) * lines
     fix_ref[...] = (bulk_ref[0] * volume - jnp.broadcast_to(flow, (8, 128))) / jnp.broadcast_to(weight, (8, 128))
@@ -444,10 +445,10 @@
             *[pltpu.VMEM(((BLOCKS + 1) * 8, 128), F32)] * 9,
             pltpu.VMEM(((BLOCKS + 1) * MSG, 128), F32),
             pltpu.VMEM((3, (BLOCKS + 1) * MSG, 128), F32),
-            pltpu.VMEM((2, 1, 128), F32),
-            pltpu.VMEM((BLOCKS * 2, 1, 128), F32),
-            pltpu.VMEM((2, 1, 128), F32),
-            pltpu.VMEM((PLANES * 2, 1, 128), F32),
+            pltpu.VMEM((1, 1, 128), F32),
+            pltpu.VMEM((BLOCKS, 1, 128), F32),
+            pltpu.VMEM((1, 1, 128), F32),
+            pltpu.VMEM((PLANES, 1, 128), F32),
             pltpu.SemaphoreType.DMA((4,)),
             pltpu.SemaphoreType.DMA((3,)),
             pltpu.SemaphoreType.DMA((9,)),

time: 27.7 us -> 27.5 us (level)
  no operation moved by 1% of the time
where the time goes in v4:
time: 27.5 us; the launch traced here: 27.4 us
  Pallas kernels  26.7 us (97%)
  between operations  0.66 us (2%)
    pallas_call x1, Pallas kernels, shards(): pl.pallas_call(reduce_kernel, name='reduce_and_solve', out_shape=[pltpu.V...  25 us
    pallas_call x1, Pallas kernels, shards(): pl.pallas_call(finish_kernel, name='finish', out_shape=jax.ShapeDtypeStru...  1.76 us

profile of v4, /device:TPU:1, one launch (start us, length us, event | category | flops | bytes accessed | tf_op | source)
XLA Modules:
  0.0 27.4 jit_solution(1270812862687296172)
XLA Ops:
  0.7 25.0 %reduce_and_solve.1 = (f32[3,16,32,512]{3,2,1,0:T(8,128)S(1)}, f32[16,32,512]{2,1,0:T(8,128)S(1)}, f32[8,128]{1,0:T(8,128)S(1)}) custom-call(f32[3,16,32,512]{3,2,1,0:T(8,128)} %velocity.1, f32[32,512]{1,0:T(8,128)} %diffusion.1, s32[32,512]{1,0:T(8,128)} %walls.1, s32[512]{0:T(512)} %stretch.1, f32[1]{0:T(128)S(6)} %copy.6.bulk), custom_call_target="tpu_custom_call" | custom-call | tf_op jit(solution)/shard_map/reduce_and_solve/pallas_call | solution.py:420
  25.6 1.8 %finish.1 = f32[3,16,32,512]{3,2,1,0:T(8,128)} custom-call(f32[3,16,32,512]{3,2,1,0:T(8,128)S(1)} %get-tuple-element.8.p_ref, f32[16,32,512]{2,1,0:T(8,128)S(1)} %get-tuple-element.9.u_ref, f32[8,128]{1,0:T(8,128)S(1)} %get-tuple-element.10.fix_ref), custom_call_target="tpu_custom_call" | custom-call | tf_op jit(solution)/shard_map/finish/pallas_call | solution.py:462

commit v5 on v4

--- a/solution.py
+++ b/solution.py
@@ -158,11 +158,11 @@
             at = a * 8 * MSG + b
             fsend[c, pl.ds(at, 8, stride=MSG), :] = part(own, a, b)
             fsend[c, pl.ds(at + 4, 8, stride=MSG), :] = part(other, a, b)
-        if c == 0:
-            pl.semaphore_wait(barrier, BLOCKS - 1 + plane)
+
+    pl.semaphore_wait(barrier, BLOCKS - 1 + plane)
+    for c in range(3):
         send_all(fsend.at[c], frecv.at[c], c)
-        if c == 0:
-            lax.fori_loop(0, plane, answer_plane, 0)
+    lax.fori_loop(0, plane, answer_plane, 0)
     local = jnp.zeros((8, 128), F32)
     for a, b in tiles_of():
         local = local + part(total, a, b)
@@ -269,17 +269,11 @@
         frecv[c, pl.ds(BLOCKS * MSG, MSG)] = zero
         wait_all(frecv.at[c], MSG, recv_sem.at[c])
 
-        def down(j, carry):
-            z, flow = carry
-            rho = frecv[c, rows8(j)] + pltpu.roll(frecv[c, rows8(j + 1)], 4, 0)
-            if c == 0:
-                flow = flow + rho * t_ref[rows8(j)]
-            z = rho * im_ref[rows8(j)] + a_ref[rows8(j)] * z
-            z_ref[rows8(j)] = z
-            return z, flow
-
-        _, flow = sweep(down, (zero, pltpu.roll(frecv[c, 0:8], 4, 0)))
+        def rhs(j):
+            return frecv[c, rows8(j)] + pltpu.roll(frecv[c, rows8(j + 1)], 4, 0)
+
         if c == 0:
+            flow = sweep(lambda j, flow: flow + rhs(j) * t_ref[rows8(j)], pltpu.roll(frecv[0, 0:8], 4, 0))
             sums = local + pltpu.roll(local, 4, 0)
             flow = jnp.sum(jnp.where(upper_half, sums - flow, 0.0), axis=0, keepdims=True)
             unit = jnp.sum(jnp.where(upper_half, weight, 0.0), axis=0, keepdims=True)
@@ -296,6 +290,13 @@
 
             lax.fori_loop(1, BLOCKS, send_flow, 0)
             flow_in[pl.ds(me, 1)] = flow_out[...]
+
+        def down(j, z):
+            z = rhs(j) * im_ref[rows8(j)] + a_ref[rows8(j)] * z
+            z_ref[rows8(j)] = z
+            return z
+
+        sweep(down, zero)
 
         def up(j, s):
             now = z_ref[rows8(j)] + g_ref[rows8(j)] * s
@@ -430,8 +431,8 @@
         scratch_shapes=[
             pltpu.VMEM((INNER,) + plane, F32),
             pltpu.VMEM((INNER,) + plane, F32),
-            pltpu.VMEM((3, BLOCKS * MSG, 128), F32),
-            pltpu.VMEM((BLOCKS * MSG, 128), F32),
+            pltpu.VMEM((3, (BLOCKS + 1) * MSG, 128), F32),
+            pltpu.VMEM(((BLOCKS + 1) * MSG, 128), F32),
             pltpu.VMEM((3, CELLS) + plane, F32),
             pltpu.VMEM(plane, F32),
             pltpu.VMEM(plane, jnp.int32),
@@ -440,7 +441,7 @@
             pltpu.VMEM((INNER,) + plane, F32),
             pltpu.VMEM((INNER,) + plane, F32),
             pltpu.VMEM((CELLS, BLOCKS, 128), F32),
-            pltpu.VMEM((3, BLOCKS * MSG, 128), F32),
+            pltpu.VMEM((3, (BLOCKS + 1) * MSG, 128), F32),
             pltpu.VMEM((3, (BLOCKS + 1) * MSG, 128), F32),
             *[pltpu.VMEM(((BLOCKS + 1) * 8, 128), F32)] * 9,
             pltpu.VMEM(((BLOCKS + 1) * MSG, 128), F32),

time: 27.5 us -> 27.5 us (level)
  no operation moved by 1% of the time
where the time goes in v5:
time: 27.5 us; the launch traced here: 27.4 us
  Pallas kernels  26.7 us (97%)
  between operations  0.66 us (2%)
    pallas_call x1, Pallas kernels, shards(): pl.pallas_call(reduce_kernel, name='reduce_and_solve', out_shape=[pltpu.V...  25 us
    pallas_call x1, Pallas kernels, shards(): pl.pallas_call(finish_kernel, name='finish', out_shape=jax.ShapeDtypeStru...  1.76 us

profile of v5, /device:TPU:1, one launch (start us, length us, event | category | flops | bytes accessed | tf_op | source)
XLA Modules:
  0.0 27.4 jit_solution(1359040415235501890)
XLA Ops:
  0.7 25.0 %reduce_and_solve.1 = (f32[3,16,32,512]{3,2,1,0:T(8,128)S(1)}, f32[16,32,512]{2,1,0:T(8,128)S(1)}, f32[8,128]{1,0:T(8,128)S(1)}) custom-call(f32[3,16,32,512]{3,2,1,0:T(8,128)} %velocity.1, f32[32,512]{1,0:T(8,128)} %diffusion.1, s32[32,512]{1,0:T(8,128)} %walls.1, s32[512]{0:T(512)} %stretch.1, f32[1]{0:T(128)S(6)} %copy.6.bulk), custom_call_target="tpu_custom_call" | custom-call | tf_op jit(solution)/shard_map/reduce_and_solve/pallas_call | solution.py:421
  25.6 1.8 %finish.1 = f32[3,16,32,512]{3,2,1,0:T(8,128)} custom-call(f32[3,16,32,512]{3,2,1,0:T(8,128)S(1)} %get-tuple-element.8.p_ref, f32[16,32,512]{2,1,0:T(8,128)S(1)} %get-tuple-element.9.u_ref, f32[8,128]{1,0:T(8,128)S(1)} %get-tuple-element.10.fix_ref), custom_call_target="tpu_custom_call" | custom-call | tf_op jit(solution)/shard_map/finish/pallas_call | solution.py:463
